TPU v7x, 32 devices: a whole 2x2x4 slice. The times are simulated.
32 devices in a mesh: dp: 16 (over z, y, x), ctx: 2 (over core).
Axes of the slice: x: 2, y: 2, z: 4, core: 2. Of those that a mesh axis runs over, the one named last changes fastest.
Arguments:
- queries: bfloat16 [4096, 4096], P(('dp', 'ctx')), may hold values from -150 to 150
- keys: bfloat16 [4096, 512], P(('dp', 'ctx')), may hold values from -4 to 4
- values: bfloat16 [4096, 512], P(('dp', 'ctx')), may hold values from -6 to 6
- lengths: int32 [32], replicated, may hold values from 1 to 512, 4096 in all
Outputs:
- attended: bfloat16 [4096, 4096], P(('dp', 'ctx'))
Inputs may be any that keep to these rules, and one draw needn't show every extreme that they name: lengths of the 32 documents sum to 4096; the largest is exactly 512.
All inputs are finite; a program needn't handle non-finite values.
Results may differ from a plain program's by a relative error of at most 0.0045.
Values may be sent and summed in bfloat16 or wider, within the bound.
No kernel may reach another device: no remote copies, remote signals or barrier semaphores. Data moves between devices by JAX's collectives and lax.ppermute only.
A program may use at most 128 MiB of HBM per device.

v0:
```python
import functools
import math

import jax
import jax.numpy as jnp
from jax import lax
from jax.experimental import pallas as pl
from jax.experimental.pallas import tpu as pltpu
from jax.sharding import PartitionSpec as P

HEAD_SIZE = 128
QUERY_HEADS = 32
KEY_VALUE_HEADS = 4
GROUP = QUERY_HEADS // KEY_VALUE_HEADS
HEADS_AT_ONCE = 4
EXCLUDED = -1e30
AXES = ("dp", "ctx")


FACTOR = math.log2(math.e) / math.sqrt(HEAD_SIZE)


def head_columns(i):
    return slice(i * HEAD_SIZE, (i + 1) * HEAD_SIZE)


def stacked(ref, heads):
    return jnp.concatenate([ref[:, head_columns(i)] for i in heads], axis=0)


def spread(ref, heads, rows, value):
    for n, i in enumerate(heads):
        ref[:, head_columns(i)] = value[n * rows : (n + 1) * rows].astype(ref.dtype)


def with_ones(value):
    return jnp.concatenate([value, jnp.ones(value.shape, value.dtype)], axis=1)


def scores_of(q, key, bias):
    scores = lax.dot_general(
        q, key, (((1,), (1,)), ((), ())), preferred_element_type=jnp.float32
    )
    return scores + jnp.concatenate([bias] * (q.shape[0] // bias.shape[0]), axis=0)


def weights_of(scores, top):
    return jnp.exp2((scores - top) * jnp.float32(FACTOR)).astype(jnp.bfloat16)


def normalised(summed, total):
    inverse = pl.reciprocal(total, approx=True)
    return summed * (inverse * (2.0 - total * inverse))


def chains():
    return [
        (range(h, h + HEADS_AT_ONCE), h // GROUP) for h in range(0, QUERY_HEADS, HEADS_AT_ONCE)
    ]


def in_turn(*stages):
    runs = chains()
    results = {}
    for turn in range(len(runs) + len(stages) - 1):
        for n, stage in enumerate(stages):
            i = turn - n
            if 0 <= i < len(runs):
                results[i] = stage(*runs[i], *results.pop(i, ()))


def pack_kernel(key_hbm, value_hbm, *refs):
    *outs, sems = refs
    rows = key_hbm.shape[0]
    copies = []
    for n, out in enumerate(outs):
        copies.append(pltpu.make_async_copy(key_hbm, out.at[:rows], sems.at[n, 0]))
        copies.append(pltpu.make_async_copy(value_hbm, out.at[rows:], sems.at[n, 1]))
    for copy in copies:
        copy.start()
    for copy in copies:
        copy.wait()


def pack(keys, values):
    rows, width = keys.shape
    packed = pltpu.VMEM((2 * rows, width), keys.dtype)
    return pl.pallas_call(
        pack_kernel,
        out_shape=(packed, packed),
        in_specs=[HBM, HBM],
        out_specs=(VMEM, VMEM),
        scratch_shapes=[pltpu.SemaphoreType.DMA((2, 2))],
        compiler_params=pltpu.CompilerParams(vmem_limit_bytes=1024 * 1024),
    )(*in_hbm(keys, values))


def own_kernel(
    rounds, rows, own_ref, lengths_hbm, q_hbm,
    _, bias_ref, needed_ref, odd_ref, q_ref, top_ref, total_ref, sum_ref,
    own_bias_ref, lengths_ref, lengths_sem, q_sems,
):
    lengths_copy = pltpu.make_async_copy(lengths_hbm, lengths_ref, lengths_sem)
    lengths_copy.start()
    width = GROUP * HEAD_SIZE
    q_copies = []
    for g in range(KEY_VALUE_HEADS):
        at = slice(g * width, (g + 1) * width)
        q_copies.append(pltpu.make_async_copy(q_hbm.at[:, at], q_ref.at[:, at], q_sems.at[g]))
        q_copies[g].start()
    me = lax.axis_index("dp") * lax.axis_size("ctx") + lax.axis_index("ctx")
    odd_ref[...] = jnp.full(odd_ref.shape, lax.rem(me, 2), jnp.int32)
    first = me * rows
    query_pos = first + lax.broadcasted_iota(jnp.int32, (rows, rows), 0)
    lengths_copy.wait()

    def later(doc, carried):
        bound, start, first_start = carried
        start = jnp.where(query_pos >= bound, bound, start)
        first_start = jnp.where(first >= bound, bound, first_start)
        return bound + lengths_ref[doc], start, first_start

    zero = jnp.int32(0)
    _, start, first_start = lax.fori_loop(
        0,
        lengths_ref.shape[0],
        later,
        (zero, jnp.zeros((rows, rows), jnp.int32), zero),
        unroll=8,
    )
    needed_ref[0] = lax.div(first - first_start + (rows - 1), jnp.int32(rows))
    lane = lax.broadcasted_iota(jnp.int32, (rows, rows), 1)

    def bias_of(allowed):
        return jnp.where(allowed, jnp.float32(0.0), jnp.float32(EXCLUDED))

    key_pos = first + lane
    own_bias_ref[...] = bias_of((key_pos >= start) & (key_pos <= query_pos))
    for b in range(2 * rounds):
        key_pos = first - (b + 1) * rows + lane
        bias_ref[:, b * rows : (b + 1) * rows] = bias_of(key_pos >= start)

    def match(heads, g):
        if heads[0] % GROUP == 0:
            q_copies[g].wait()
        return (scores_of(stacked(q_ref, heads), own_ref[:rows, head_columns(g)], own_bias_ref[...]),)

    def weigh(heads, g, scores):
        top = jnp.max(scores, axis=1, keepdims=True)
        spread(top_ref, heads, rows, jnp.broadcast_to(top, scores.shape))
        return (weights_of(scores, top),)

    def gather(heads, g, weights):
        value = with_ones(own_ref[rows:, head_columns(g)])
        summed = jnp.dot(weights, value, preferred_element_type=jnp.float32)
        spread(sum_ref, heads, rows, summed[:, :HEAD_SIZE])
        spread(total_ref, heads, rows, summed[:, HEAD_SIZE:])

    in_turn(match, weigh, gather)


def in_vmem(*operands):
    return [pltpu.with_memory_space_constraint(x, pltpu.VMEM) for x in operands]


def in_hbm(*operands):
    return [pltpu.with_memory_space_constraint(x, pltpu.HBM) for x in operands]


SMEM = pl.BlockSpec(memory_space=pltpu.SMEM)
VMEM = pl.BlockSpec(memory_space=pltpu.VMEM)
HBM = pl.BlockSpec(memory_space=pltpu.HBM)


def own_part(lengths, queries, own, rounds):
    rows = queries.shape[0]
    partial = pltpu.VMEM(queries.shape, jnp.float32)
    return pl.pallas_call(
        functools.partial(own_kernel, rounds, rows),
        out_shape=(
            pltpu.VMEM(own.shape, own.dtype),
            pltpu.VMEM((rows, 2 * rounds * rows), jnp.float32),
            jax.ShapeDtypeStruct((1,), jnp.int32),
            pltpu.VMEM((1, own.shape[1]), jnp.int32),
            pltpu.VMEM(queries.shape, queries.dtype),
            partial,
            partial,
            partial,
        ),
        in_specs=[VMEM, HBM, HBM],
        out_specs=(VMEM, VMEM, SMEM, VMEM, VMEM, VMEM, VMEM, VMEM),
        input_output_aliases={0: 0},
        scratch_shapes=[
            pltpu.VMEM((rows, rows), jnp.float32),
            pltpu.SMEM(lengths.shape, jnp.int32),
            pltpu.SemaphoreType.DMA,
            pltpu.SemaphoreType.DMA((KEY_VALUE_HEADS,)),
        ],
        compiler_params=pltpu.CompilerParams(vmem_limit_bytes=10 * 1024 * 1024),
        cost_estimate=pl.CostEstimate(
            flops=4 * 10**9, bytes_accessed=16 * 10**6, transcendentals=rows * queries.size
        ),
    )(*in_vmem(own), *in_hbm(lengths, queries))


def behind_kernel(
    before, last, rows, needed_ref, bias_ref, q_ref, *refs
):
    width = GROUP * HEAD_SIZE
    beyond = needed_ref[0] - before
    *near_refs, further_ref, top_ref, total_ref, sum_ref = refs[: 5 if last else 6]
    refs = refs[5 if last else 6 :]
    if last:
        near_refs = (near_refs[0].at[:rows], near_refs[0].at[rows:])
    pairs = (near_refs, (further_ref.at[:rows], further_ref.at[rows:]))
    if last:
        out_hbm, out_ref, out_sems = refs

        def out_copy(g):
            at = slice(g * width, (g + 1) * width)
            return pltpu.make_async_copy(out_ref.at[:, at], out_hbm.at[:, at], out_sems.at[g])

    else:
        _, new_top_ref, new_total_ref, new_sum_ref = refs

    def finish(heads, g, summed, total):
        if last:
            spread(out_ref, heads, rows, normalised(summed, total))
            if heads[-1] % GROUP == GROUP - 1:
                out_copy(g).start()
        else:
            spread(new_sum_ref, heads, rows, summed)
            spread(new_total_ref, heads, rows, total)

    def attend(count):
        def match(heads, g):
            key = jnp.concatenate([key[:, head_columns(g)] for key, _ in pairs[:count]], axis=0)
            bias = bias_ref[:, before * rows : (before + count) * rows]
            return (scores_of(stacked(q_ref, heads), key, bias),)

        def weigh(heads, g, scores):
            old_top = stacked(top_ref, heads)
            top = jnp.maximum(old_top, jnp.max(scores, axis=1, keepdims=True))
            fade = jnp.exp2((old_top - top) * jnp.float32(FACTOR))
            if not last:
                spread(new_top_ref, heads, rows, top)
            return weights_of(scores, jnp.concatenate([top] * count, axis=1)), fade

        def gather(heads, g, weights, fade):
            value = jnp.concatenate([value[:, head_columns(g)] for _, value in pairs[:count]], axis=0)
            more = jnp.dot(weights, with_ones(value), preferred_element_type=jnp.float32)
            summed = stacked(sum_ref, heads) * fade + more[:, :HEAD_SIZE]
            total = stacked(total_ref, heads) * fade + more[:, HEAD_SIZE:]
            finish(heads, g, summed, total)

        in_turn(match, weigh, gather)

    @pl.when(beyond > 1)
    def _():
        attend(2)

    @pl.when(beyond == 1)
    def _():
        attend(1)

    if last:
        @pl.when(beyond < 1)
        def _():
            in_turn(
                lambda heads, g: finish(heads, g, stacked(sum_ref, heads), stacked(total_ref, heads))
            )

        for g in range(KEY_VALUE_HEADS):
            out_copy(g).wait()


def behind_part(before, last, needed, bias, queries, halves, further, parts):
    rows = queries.shape[0]
    area = rows * rows * 2 * QUERY_HEADS
    operands = in_vmem(bias, queries, *halves, further, *parts)
    if last:
        out_shape = jax.ShapeDtypeStruct(queries.shape, queries.dtype)
        out_specs = HBM
        scratch = [
            pltpu.VMEM(queries.shape, queries.dtype),
            pltpu.SemaphoreType.DMA((KEY_VALUE_HEADS,)),
        ]
        aliases = {}
    else:
        kept = (further, *parts)
        out_shape = tuple(pltpu.VMEM(part.shape, part.dtype) for part in kept)
        out_specs = (VMEM,) * len(kept)
        scratch = []
        aliases = {5 + n: n for n in range(len(kept))}
    return pl.pallas_call(
        functools.partial(behind_kernel, before, last, rows),
        out_shape=out_shape,
        in_specs=[SMEM] + [VMEM] * len(operands),
        out_specs=out_specs,
        scratch_shapes=scratch,
        input_output_aliases=aliases,
        compiler_params=pltpu.CompilerParams(vmem_limit_bytes=10 * 1024 * 1024),
        cost_estimate=pl.CostEstimate(
            flops=4 * area, bytes_accessed=queries.size, transcendentals=0
        ),
    )(needed, *operands)


def per_device(queries, keys, values, lengths):
    count = lax.axis_size("dp") * lax.axis_size("ctx")
    rounds = lax.axis_size("ctx")

    def from_behind(block, r):
        by = 2 * (r + 1)
        return lax.ppermute(block, AXES, [(i, i + by) for i in range(count - by)])

    packed, own = pack(keys, values)
    fetched = [from_behind(packed, 0)]
    own, bias, needed, odd, queries, *parts = own_part(lengths, queries, own, rounds)
    fetched += [from_behind(own, r) for r in range(1, rounds)]
    swap = [(i, i ^ 1) for i in range(count)]
    nearer = own
    for r, further in enumerate(fetched):
        last = r == rounds - 1
        cuts = 1 if last else 2
        halves = []
        for old, new in zip(jnp.split(nearer, cuts), jnp.split(further, cuts)):
            halves.append(lax.ppermute(jnp.where(odd == 1, new, old), AXES, swap))
        result = behind_part(2 * r, last, needed, bias, queries, halves, further, parts)
        if not last:
            nearer, *parts = result
    return result


def solution(mesh):
    in_specs = (P(AXES, None), P(AXES, None), P(AXES, None), P())
    return jax.shard_map(
        per_device, mesh=mesh, in_specs=in_specs, out_specs=P(AXES, None), check_vma=False
    )
```

profile of v0, /device:TPU:9, one launch (start us, length us, event | category | flops | bytes accessed | tf_op | source)
XLA Modules:
  0.0 24.8 jit_solution(7190453138668290847)
XLA Ops:
  0.0 1.1 %shard_map.46 = (bf16[256,512]{1,0:T(8,128)(2,1)S(1)}, bf16[256,512]{1,0:T(8,128)(2,1)S(1)}) custom-call(bf16[128,512]{1,0:T(8,128)(2,1)} %key_hbm.1, bf16[128,512]{1,0:T(8,128)(2,1)} %value_hbm.1), custom_call_target="tpu_custom_call" | custom-call | tf_op jit(solution)/shard_map/pallas_call | solution.py:88
  1.1 3.1 %collective-permute-start.1 = (bf16[256,512]{1,0:T(8,128)(2,1)S(1)}, bf16[256,512]{1,0:T(8,128)(2,1)S(1)}, u32[]{:S(2)}, u32[]{:S(2)}) collective-permute-start(bf16[256,512]{1,0:T(8,128)(2,1)S(1)} %get-tuple-element.25), channel_id=1, source_target_pairs={{0,2},{1,3},{2,4},{3,5},{4,6},{5,7},{6,8},{7,9},{8,10},{9,11},{10,... | collective-permute-start | bytes 786440 | tf_op jit(solution)/shard_map/ppermute | solution.py:315
  4.3 2.8 %shard_map.47 = (bf16[256,512]{1,0:T(8,128)(2,1)S(1)}, f32[128,512]{1,0:T(8,128)S(1)}, s32[1]{0:T(128)}, s32[1,512]{1,0:T(1,128)S(1)}, bf16[128,4096]{1,0:T(8,12...) custom-call(bf16[256,512]{1,0:T(8,128)(2,1)S(1)} %get-tuple-element., ...), custom_call_target="tpu_custom_call", output_to_operand_aliasing={{0}: (0, {})} | custom-call | flops 4000000000 | bytes 16000000 | tf_op jit(solution)/shard_map/pallas_call | solution.py:178
  7.1 3.1 %collective-permute-start = (bf16[256,512]{1,0:T(8,128)(2,1)S(1)}, bf16[256,512]{1,0:T(8,128)(2,1)S(1)}, u32[]{:S(2)}, u32[]{:S(2)}) collective-permute-start(bf16[256,512]{1,0:T(8,128)(2,1)S(1)} %get-tuple-element.24), channel_id=1, source_target_pairs={{0,4},{1,5},{2,6},{3,7},{4,8},{5,9},{6,10},{7,11},{8,12},{9,13},{1... | collective-permute-start | bytes 786440 | tf_op jit(solution)/shard_map/ppermute | solution.py:315
  10.3 1.7 %collective-permute-done.1.refs_2_ = bf16[256,512]{1,0:T(8,128)(2,1)S(1)} collective-permute-done((bf16[256,512]{1,0:T(8,128)(2,1)S(1)}, bf16[256,512]{1,0:T(8,128)(2,1)S(1)}, u32[]{:S(2)}, u32[]{:S(2)}) %collective-permute-start.1) | collective-permute-done | bytes 262176 | tf_op jit(solution)/shard_map/ppermute | solution.py:315
  12.0 2.2 %collective-permute-start.3 = (bf16[128,512]{1,0:T(8,128)(2,1)S(1)}, bf16[128,512]{1,0:T(8,128)(2,1)S(1)}, u32[]{:S(2)}, u32[]{:S(2)}) collective-permute-start(bf16[128,512]{1,0:T(8,128)(2,1)S(1)} %get-tuple-element.33), channel_id=1, source_target_pairs={{0,1},{1,0},{2,3},{3,2},{4,5},{5,4},{6,7},{7,6},{8,9},{9,8},{10,11... | collective-permute-start | bytes 393224 | tf_op jit(solution)/shard_map/ppermute | solution.py:328
  14.2 0.1 collective-permute-start.2
  14.3 0.9 %collective-permute-done.3.refs_1_ = bf16[128,512]{1,0:T(8,128)(2,1)S(1)} collective-permute-done((bf16[128,512]{1,0:T(8,128)(2,1)S(1)}, bf16[128,512]{1,0:T(8,128)(2,1)S(1)}, u32[]{:S(2)}, u32[]{:S(2)}) %collective-permute-start.3) | collective-permute-done | bytes 131104 | tf_op jit(solution)/shard_map/ppermute | solution.py:328
  15.2 0.4 %collective-permute-done.2.refs_0_ = bf16[128,512]{1,0:T(8,128)(2,1)S(1)} collective-permute-done((bf16[128,512]{1,0:T(8,128)(2,1)S(1)}, bf16[128,512]{1,0:T(8,128)(2,1)S(1)}, u32[]{:S(2)}, u32[]{:S(2)}) %collective-permute-start.2) | collective-permute-done | bytes 131104 | tf_op jit(solution)/shard_map/ppermute | solution.py:328
  15.5 3.7 %shard_map.48 = (bf16[256,512]{1,0:T(8,128)(2,1)S(1)}, f32[128,4096]{1,0:T(8,128)S(1)}, f32[128,4096]{1,0:T(8,128)S(1)}, f32[128,4096]{1,0:T(8,128)S(1)}) custom-call(s32[1]{0:T(128)} %get-tuple-element.20.needed_ref, f32[128,512]{1,0:T(8,128)S(1)} %get-tuple-element.21.bias_ref, ...), custom_call_target="tpu_custom_call", output_to_operand_aliasing={{0}: (5, {}), {1}: (6, {}), {2}: (7, {}), {3}: (8, {})} | custom-call | flops 4194304 | bytes 524288 | tf_op jit(solution)/shard_map/pallas_call | solution.py:295
  19.2 0.0 collective-permute-done.refs_1_
  19.3 0.3 %collective-permute-start.4 = (bf16[256,512]{1,0:T(8,128)(2,1)S(1)}, bf16[256,512]{1,0:T(8,128)(2,1)S(1)}, u32[]{:S(2)}, u32[]{:S(2)}) collective-permute-start(bf16[256,512]{1,0:T(8,128)(2,1)S(1)} %broadcast_select_fusion), channel_id=1, source_target_pairs={{0,1},{1,0},{2,3},{3,2},{4,5},{5,4},{6,7},{7,6},{8,9},{9,8},{10,11... | collective-permute-start | bytes 786440 | tf_op jit(solution)/shard_map/ppermute | solution.py:328
  19.5 1.3 %collective-permute-done.4.refs_0_ = bf16[256,512]{1,0:T(8,128)(2,1)S(1)} collective-permute-done((bf16[256,512]{1,0:T(8,128)(2,1)S(1)}, bf16[256,512]{1,0:T(8,128)(2,1)S(1)}, u32[]{:S(2)}, u32[]{:S(2)}) %collective-permute-start.4) | collective-permute-done | bytes 262176 | tf_op jit(solution)/shard_map/ppermute | solution.py:328
  20.9 3.9 %shard_map.49 = bf16[128,4096]{1,0:T(8,128)(2,1)} custom-call(s32[1]{0:T(128)} %get-tuple-element.20.needed_ref, f32[128,512]{1,0:T(8,128)S(1)} %get-tuple-element.21.bias_ref, bf16[128,4096]{1,0:T(8,128)(2,1)S(1)} %get-tuple-element.22.q_ref, bf16[256,512]{1,0:T(8,128)(2,1)S(1)} %collective-permute-done.4.refs_0_, ...), custom_call_target="tpu_custom_call" | custom-call | flops 4194304 | bytes 524288 | tf_op jit(solution)/shard_map/pallas_call | solution.py:295
  (3 shorter events, 0.1 us)
Async XLA Ops:
  1.1 10.9 %collective-permute-start.1 = (bf16[256,512]{1,0:T(8,128)(2,1)S(1)}, bf16[256,512]{1,0:T(8,128)(2,1)S(1)}, u32[]{:S(2)}, u32[]{:S(2)}) collective-permute-start(bf16[256,512]{1,0:T(8,128)(2,1)S(1)} %get-tuple-element.25), channel_id=1, source_target_pairs={{0,2},{1,3},{2,4},{3,5},{4,6},{5,7},{6,8},{7,9},{8,10},{9,11},{10,... | collective-permute-start | bytes 786440 | tf_op jit(solution)/shard_map/ppermute | solution.py:315
  7.1 12.1 %collective-permute-start = (bf16[256,512]{1,0:T(8,128)(2,1)S(1)}, bf16[256,512]{1,0:T(8,128)(2,1)S(1)}, u32[]{:S(2)}, u32[]{:S(2)}) collective-permute-start(bf16[256,512]{1,0:T(8,128)(2,1)S(1)} %get-tuple-element.24), channel_id=1, source_target_pairs={{0,4},{1,5},{2,6},{3,7},{4,8},{5,9},{6,10},{7,11},{8,12},{9,13},{1... | collective-permute-start | bytes 786440 | tf_op jit(solution)/shard_map/ppermute | solution.py:315
  12.0 3.1 %collective-permute-start.3 = (bf16[128,512]{1,0:T(8,128)(2,1)S(1)}, bf16[128,512]{1,0:T(8,128)(2,1)S(1)}, u32[]{:S(2)}, u32[]{:S(2)}) collective-permute-start(bf16[128,512]{1,0:T(8,128)(2,1)S(1)} %get-tuple-element.33), channel_id=1, source_target_pairs={{0,1},{1,0},{2,3},{3,2},{4,5},{5,4},{6,7},{7,6},{8,9},{9,8},{10,11... | collective-permute-start | bytes 393224 | tf_op jit(solution)/shard_map/ppermute | solution.py:328
  14.2 1.3 %collective-permute-start.2 = (bf16[128,512]{1,0:T(8,128)(2,1)S(1)}, bf16[128,512]{1,0:T(8,128)(2,1)S(1)}, u32[]{:S(2)}, u32[]{:S(2)}) collective-permute-start(bf16[128,512]{1,0:T(8,128)(2,1)S(1)} %get-tuple-element.34), channel_id=1, source_target_pairs={{0,1},{1,0},{2,3},{3,2},{4,5},{5,4},{6,7},{7,6},{8,9},{9,8},{10,11... | collective-permute-start | bytes 393224 | tf_op jit(solution)/shard_map/ppermute | solution.py:328
  19.3 1.6 %collective-permute-start.4 = (bf16[256,512]{1,0:T(8,128)(2,1)S(1)}, bf16[256,512]{1,0:T(8,128)(2,1)S(1)}, u32[]{:S(2)}, u32[]{:S(2)}) collective-permute-start(bf16[256,512]{1,0:T(8,128)(2,1)S(1)} %broadcast_select_fusion), channel_id=1, source_target_pairs={{0,1},{1,0},{2,3},{3,2},{4,5},{5,4},{6,7},{7,6},{8,9},{9,8},{10,11... | collective-permute-start | bytes 786440 | tf_op jit(solution)/shard_map/ppermute | solution.py:328
where the time goes:
time: 24.5 us; the launch traced here: 24.8 us
  Pallas kernels  11.5 us (47%)
  starting transfers between devices  8.76 us (36%)
  waiting for transfers between devices  4.34 us (18%)
    pallas_call x2, Pallas kernels, behind_part(): pl.pallas_call(functools.partial(behind_kernel, before, last, rows), out_...  7.58 us
    ppermute x2, starting transfers between devices, from_behind(): return lax.ppermute(block, AXES, [(i, i + by) for i in range(count - by)])  6.27 us
    pallas_call x1, Pallas kernels, own_part(): pl.pallas_call(functools.partial(own_kernel, rounds, rows), out_shape=(pl...  2.83 us
    ppermute x3, waiting for transfers between devices, per_device(): halves.append(lax.ppermute(jnp.where(odd == 1, new, old), AXES, swap))  2.61 us
    ppermute x3, starting transfers between devices, per_device(): halves.append(lax.ppermute(jnp.where(odd == 1, new, old), AXES, swap))  2.49 us
    ppermute x2, waiting for transfers between devices, from_behind(): return lax.ppermute(block, AXES, [(i, i + by) for i in range(count - by)])  1.72 us
    pallas_call x1, Pallas kernels, pack(): pl.pallas_call(pack_kernel, out_shape=(packed, packed), in_specs=[HBM, HB...  1.13 us
  transfers between devices with their start and end apart: 5, of which 4 were waited for; matrix products, arithmetic and copies ran while one was open for 0% of the time, Pallas kernels for 26%

commit v1 on v0

--- a/solution.py
+++ b/solution.py
@@ -14,6 +14,7 @@
 GROUP = QUERY_HEADS // KEY_VALUE_HEADS
 HEADS_AT_ONCE = 4
 EXCLUDED = -1e30
+PAD = 16
 AXES = ("dp", "ctx")
 
 
@@ -75,7 +76,7 @@
     copies = []
     for n, out in enumerate(outs):
         copies.append(pltpu.make_async_copy(key_hbm, out.at[:rows], sems.at[n, 0]))
-        copies.append(pltpu.make_async_copy(value_hbm, out.at[rows:], sems.at[n, 1]))
+        copies.append(pltpu.make_async_copy(value_hbm, out.at[rows : 2 * rows], sems.at[n, 1]))
     for copy in copies:
         copy.start()
     for copy in copies:
@@ -85,9 +86,10 @@
 def pack(keys, values):
     rows, width = keys.shape
     packed = pltpu.VMEM((2 * rows, width), keys.dtype)
+    longer = pltpu.VMEM((2 * rows + PAD, width), keys.dtype)
     return pl.pallas_call(
         pack_kernel,
-        out_shape=(packed, packed),
+        out_shape=(packed, longer),
         in_specs=[HBM, HBM],
         out_specs=(VMEM, VMEM),
         scratch_shapes=[pltpu.SemaphoreType.DMA((2, 2))],
@@ -97,7 +99,7 @@
 
 def own_kernel(
     rounds, rows, own_ref, lengths_hbm, q_hbm,
-    _, bias_ref, needed_ref, odd_ref, q_ref, top_ref, total_ref, sum_ref,
+    longer_ref, bias_ref, needed_ref, odd_ref, q_ref, top_ref, total_ref, sum_ref,
     own_bias_ref, lengths_ref, lengths_sem, q_sems,
 ):
     lengths_copy = pltpu.make_async_copy(lengths_hbm, lengths_ref, lengths_sem)
@@ -109,6 +111,7 @@
         q_copies.append(pltpu.make_async_copy(q_hbm.at[:, at], q_ref.at[:, at], q_sems.at[g]))
         q_copies[g].start()
     me = lax.axis_index("dp") * lax.axis_size("ctx") + lax.axis_index("ctx")
+    longer_ref[2 * rows :, :] = jnp.zeros((PAD, longer_ref.shape[1]), longer_ref.dtype)
     odd_ref[...] = jnp.full(odd_ref.shape, lax.rem(me, 2), jnp.int32)
     first = me * rows
     query_pos = first + lax.broadcasted_iota(jnp.int32, (rows, rows), 0)
@@ -128,7 +131,8 @@
         (zero, jnp.zeros((rows, rows), jnp.int32), zero),
         unroll=8,
     )
-    needed_ref[0] = lax.div(first - first_start + (rows - 1), jnp.int32(rows))
+    needed = lax.div(first - first_start + (rows - 1), jnp.int32(rows))
+    needed_ref[...] = jnp.full(needed_ref.shape, needed, jnp.int32)
     lane = lax.broadcasted_iota(jnp.int32, (rows, rows), 1)
 
     def bias_of(allowed):
@@ -151,7 +155,7 @@
         return (weights_of(scores, top),)
 
     def gather(heads, g, weights):
-        value = with_ones(own_ref[rows:, head_columns(g)])
+        value = with_ones(own_ref[rows : 2 * rows, head_columns(g)])
         summed = jnp.dot(weights, value, preferred_element_type=jnp.float32)
         spread(sum_ref, heads, rows, summed[:, :HEAD_SIZE])
         spread(total_ref, heads, rows, summed[:, HEAD_SIZE:])
@@ -180,7 +184,7 @@
         out_shape=(
             pltpu.VMEM(own.shape, own.dtype),
             pltpu.VMEM((rows, 2 * rounds * rows), jnp.float32),
-            jax.ShapeDtypeStruct((1,), jnp.int32),
+            pltpu.VMEM((8, 128), jnp.int32),
             pltpu.VMEM((1, own.shape[1]), jnp.int32),
             pltpu.VMEM(queries.shape, queries.dtype),
             partial,
@@ -188,7 +192,7 @@
             partial,
         ),
         in_specs=[VMEM, HBM, HBM],
-        out_specs=(VMEM, VMEM, SMEM, VMEM, VMEM, VMEM, VMEM, VMEM),
+        out_specs=(VMEM,) * 8,
         input_output_aliases={0: 0},
         scratch_shapes=[
             pltpu.VMEM((rows, rows), jnp.float32),
@@ -204,15 +208,11 @@
 
 
 def behind_kernel(
-    before, last, rows, needed_ref, bias_ref, q_ref, *refs
+    before, last, rows, needed_ref, bias_ref, q_ref, near_ref, further_ref, top_ref, total_ref, sum_ref, *refs
 ):
     width = GROUP * HEAD_SIZE
-    beyond = needed_ref[0] - before
-    *near_refs, further_ref, top_ref, total_ref, sum_ref = refs[: 5 if last else 6]
-    refs = refs[5 if last else 6 :]
-    if last:
-        near_refs = (near_refs[0].at[:rows], near_refs[0].at[rows:])
-    pairs = (near_refs, (further_ref.at[:rows], further_ref.at[rows:]))
+    beyond = needed_ref[0, 0] - before
+    pairs = [(ref.at[:rows], ref.at[rows : 2 * rows]) for ref in (near_ref, further_ref)]
     if last:
         out_hbm, out_ref, out_sems = refs
 
@@ -274,10 +274,10 @@
             out_copy(g).wait()
 
 
-def behind_part(before, last, needed, bias, queries, halves, further, parts):
+def behind_part(before, last, needed, bias, queries, near, further, parts):
     rows = queries.shape[0]
     area = rows * rows * 2 * QUERY_HEADS
-    operands = in_vmem(bias, queries, *halves, further, *parts)
+    operands = in_vmem(needed, bias, queries, near, further, *parts)
     if last:
         out_shape = jax.ShapeDtypeStruct(queries.shape, queries.dtype)
         out_specs = HBM
@@ -291,11 +291,11 @@
         out_shape = tuple(pltpu.VMEM(part.shape, part.dtype) for part in kept)
         out_specs = (VMEM,) * len(kept)
         scratch = []
-        aliases = {5 + n: n for n in range(len(kept))}
+        aliases = {4 + n: n for n in range(len(kept))}
     return pl.pallas_call(
         functools.partial(behind_kernel, before, last, rows),
         out_shape=out_shape,
-        in_specs=[SMEM] + [VMEM] * len(operands),
+        in_specs=[VMEM] * len(operands),
         out_specs=out_specs,
         scratch_shapes=scratch,
         input_output_aliases=aliases,
@@ -303,7 +303,7 @@
         cost_estimate=pl.CostEstimate(
             flops=4 * area, bytes_accessed=queries.size, transcendentals=0
         ),
-    )(needed, *operands)
+    )(*operands)
 
 
 def per_device(queries, keys, values, lengths):
@@ -320,13 +320,11 @@
     fetched += [from_behind(own, r) for r in range(1, rounds)]
     swap = [(i, i ^ 1) for i in range(count)]
     nearer = own
+    size = 2 * keys.shape[0]
     for r, further in enumerate(fetched):
         last = r == rounds - 1
-        cuts = 1 if last else 2
-        halves = []
-        for old, new in zip(jnp.split(nearer, cuts), jnp.split(further, cuts)):
-            halves.append(lax.ppermute(jnp.where(odd == 1, new, old), AXES, swap))
-        result = behind_part(2 * r, last, needed, bias, queries, halves, further, parts)
+        near = lax.ppermute(jnp.where(odd == 1, further[:size], nearer[:size]), AXES, swap)
+        result = behind_part(2 * r, last, needed, bias, queries, near, further, parts)
         if not last:
             nearer, *parts = result
     return result

time: 24.5 us -> 24 us (0.980)
  the two profiles are of different devices: /device:TPU:9 before, /device:TPU:25 now
where the time goes in v1:
time: 24 us; the launch traced here: 24.1 us
  Pallas kernels  10.2 us (42%)
  starting transfers between devices  9.62 us (40%)
  waiting for transfers between devices  4.05 us (17%)
    pallas_call x2, Pallas kernels, behind_part(): pl.pallas_call(functools.partial(behind_kernel, before, last, rows), out_...  6.28 us
    ppermute x2, starting transfers between devices, from_behind(): return lax.ppermute(block, AXES, [(i, i + by) for i in range(count - by)])  6.27 us
    ppermute x2, starting transfers between devices, per_device(): lax.ppermute(jnp.where(odd == 1, further[:size], nearer[:size]), AXES, swap)  3.35 us
    pallas_call x1, Pallas kernels, own_part(): pl.pallas_call(functools.partial(own_kernel, rounds, rows), out_shape=(pl...  2.83 us
    ppermute x2, waiting for transfers between devices, per_device(): lax.ppermute(jnp.where(odd == 1, further[:size], nearer[:size]), AXES, swap)  2.32 us
    ppermute x2, waiting for transfers between devices, from_behind(): return lax.ppermute(block, AXES, [(i, i + by) for i in range(count - by)])  1.72 us
    pallas_call x1, Pallas kernels, pack(): pl.pallas_call(pack_kernel, out_shape=(packed, longer), in_specs=[HBM, HB...  1.13 us
  transfers between devices with their start and end apart: 4, of which 3 were waited for; matrix products, arithmetic and copies ran while one was open for 0% of the time, Pallas kernels for 24%

profile of v1, /device:TPU:25, one launch (start us, length us, event | category | flops | bytes accessed | tf_op | source)
XLA Modules:
  0.0 24.1 jit_solution(4764967365376380066)
XLA Ops:
  0.0 1.1 %shard_map.46 = (bf16[256,512]{1,0:T(8,128)(2,1)S(1)}, bf16[272,512]{1,0:T(8,128)(2,1)S(1)}) custom-call(bf16[128,512]{1,0:T(8,128)(2,1)} %key_hbm.1, bf16[128,512]{1,0:T(8,128)(2,1)} %value_hbm.1), custom_call_target="tpu_custom_call" | custom-call | tf_op jit(solution)/shard_map/pallas_call | solution.py:90
  1.1 3.1 %collective-permute-start.1 = (bf16[256,512]{1,0:T(8,128)(2,1)S(1)}, bf16[256,512]{1,0:T(8,128)(2,1)S(1)}, u32[]{:S(2)}, u32[]{:S(2)}) collective-permute-start(bf16[256,512]{1,0:T(8,128)(2,1)S(1)} %get-tuple-element.25), channel_id=1, source_target_pairs={{0,2},{1,3},{2,4},{3,5},{4,6},{5,7},{6,8},{7,9},{8,10},{9,11},{10,... | collective-permute-start | bytes 786440 | tf_op jit(solution)/shard_map/ppermute | solution.py:315
  4.3 2.8 %shard_map.47 = (bf16[272,512]{1,0:T(8,128)(2,1)S(1)}, f32[128,512]{1,0:T(8,128)S(1)}, s32[8,128]{1,0:T(8,128)S(1)}, s32[1,512]{1,0:T(1,128)S(1)}, bf16[128,4096...) custom-call(bf16[272,512]{1,0:T(8,128)(2,1)S(1)} %get-tuple-element., ...), custom_call_target="tpu_custom_call", output_to_operand_aliasing={{0}: (0, {})} | custom-call | flops 4000000000 | bytes 16000000 | tf_op jit(solution)/shard_map/pallas_call | solution.py:182
  7.1 3.1 %collective-permute-start = (bf16[272,512]{1,0:T(8,128)(2,1)S(1)}, bf16[272,512]{1,0:T(8,128)(2,1)S(1)}, u32[]{:S(2)}, u32[]{:S(2)}) collective-permute-start(bf16[272,512]{1,0:T(8,128)(2,1)S(1)} %get-tuple-element.24), channel_id=1, source_target_pairs={{0,4},{1,5},{2,6},{3,7},{4,8},{5,9},{6,10},{7,11},{8,12},{9,13},{1... | collective-permute-start | bytes 835592 | tf_op jit(solution)/shard_map/ppermute | solution.py:315
  10.3 1.7 %collective-permute-done.1.further_ref = bf16[256,512]{1,0:T(8,128)(2,1)S(1)} collective-permute-done((bf16[256,512]{1,0:T(8,128)(2,1)S(1)}, bf16[256,512]{1,0:T(8,128)(2,1)S(1)}, u32[]{:S(2)}, u32[]{:S(2)}) %collective-permute-start.1) | collective-permute-done | bytes 262176 | tf_op jit(solution)/shard_map/ppermute | solution.py:315
  12.0 2.2 %collective-permute-start.2 = (bf16[256,512]{1,0:T(8,128)(2,1)S(1)}, bf16[256,512]{1,0:T(8,128)(2,1)S(1)}, u32[]{:S(2)}, u32[]{:S(2)}) collective-permute-start(bf16[256,512]{1,0:T(8,128)(2,1)S(1)} %slice_select_fusion.1), channel_id=1, source_target_pairs={{0,1},{1,0},{2,3},{3,2},{4,5},{5,4},{6,7},{7,6},{8,9},{9,8},{10,11... | collective-permute-start | bytes 786440 | tf_op jit(solution)/shard_map/ppermute | solution.py:326
  14.2 1.2 %collective-permute-done.2.near_ref = bf16[256,512]{1,0:T(8,128)(2,1)S(1)} collective-permute-done((bf16[256,512]{1,0:T(8,128)(2,1)S(1)}, bf16[256,512]{1,0:T(8,128)(2,1)S(1)}, u32[]{:S(2)}, u32[]{:S(2)}) %collective-permute-start.2) | collective-permute-done | bytes 262176 | tf_op jit(solution)/shard_map/ppermute | solution.py:326
  15.4 3.0 %shard_map.48 = (bf16[256,512]{1,0:T(8,128)(2,1)S(1)}, f32[128,4096]{1,0:T(8,128)S(1)}, f32[128,4096]{1,0:T(8,128)S(1)}, f32[128,4096]{1,0:T(8,128)S(1)}) custom-call(s32[8,128]{1,0:T(8,128)S(1)} %get-tuple-element.20.needed_ref, f32[128,512]{1,0:T(8,128)S(1)} %get-tuple-element.21.bias_ref, ...), custom_call_target="tpu_custom_call", output_to_operand_aliasing={{0}: (4, {}), {1}: (5, {}), {2}: (6, {}), {3}: (7, {})} | custom-call | flops 4194304 | bytes 524288 | tf_op jit(solution)/shard_map/pallas_call | solution.py:295
  18.4 0.0 collective-permute-done.further_ref
  18.4 1.2 %collective-permute-start.3 = (bf16[256,512]{1,0:T(8,128)(2,1)S(1)}, bf16[256,512]{1,0:T(8,128)(2,1)S(1)}, u32[]{:S(2)}, u32[]{:S(2)}) collective-permute-start(bf16[256,512]{1,0:T(8,128)(2,1)S(1)} %slice_select_fusion), channel_id=1, source_target_pairs={{0,1},{1,0},{2,3},{3,2},{4,5},{5,4},{6,7},{7,6},{8,9},{9,8},{10,11... | collective-permute-start | bytes 786440 | tf_op jit(solution)/shard_map/ppermute | solution.py:326
  19.6 1.2 %collective-permute-done.3.near_ref = bf16[256,512]{1,0:T(8,128)(2,1)S(1)} collective-permute-done((bf16[256,512]{1,0:T(8,128)(2,1)S(1)}, bf16[256,512]{1,0:T(8,128)(2,1)S(1)}, u32[]{:S(2)}, u32[]{:S(2)}) %collective-permute-start.3) | collective-permute-done | bytes 262176 | tf_op jit(solution)/shard_map/ppermute | solution.py:326
  20.8 3.3 %shard_map.49 = bf16[128,4096]{1,0:T(8,128)(2,1)} custom-call(s32[8,128]{1,0:T(8,128)S(1)} %get-tuple-element.20.needed_ref, f32[128,512]{1,0:T(8,128)S(1)} %get-tuple-element.21.bias_ref, bf16[128,4096]{1,0:T(8,128)(2,1)S(1)} %get-tuple-element.22.q_ref, bf16[256,512]{1,0:T(8,128)(2,1)S(1)} %collective-permute-done.3.near_ref, ...), custom_call_target="tpu_custom_call" | custom-call | flops 4194304 | bytes 524288 | tf_op jit(solution)/shard_map/pallas_call | solution.py:295
  (3 shorter events, 0.1 us)
Async XLA Ops:
  1.1 10.9 %collective-permute-start.1 = (bf16[256,512]{1,0:T(8,128)(2,1)S(1)}, bf16[256,512]{1,0:T(8,128)(2,1)S(1)}, u32[]{:S(2)}, u32[]{:S(2)}) collective-permute-start(bf16[256,512]{1,0:T(8,128)(2,1)S(1)} %get-tuple-element.25), channel_id=1, source_target_pairs={{0,2},{1,3},{2,4},{3,5},{4,6},{5,7},{6,8},{7,9},{8,10},{9,11},{10,... | collective-permute-start | bytes 786440 | tf_op jit(solution)/shard_map/ppermute | solution.py:315
  7.1 11.3 %collective-permute-start = (bf16[272,512]{1,0:T(8,128)(2,1)S(1)}, bf16[272,512]{1,0:T(8,128)(2,1)S(1)}, u32[]{:S(2)}, u32[]{:S(2)}) collective-permute-start(bf16[272,512]{1,0:T(8,128)(2,1)S(1)} %get-tuple-element.24), channel_id=1, source_target_pairs={{0,4},{1,5},{2,6},{3,7},{4,8},{5,9},{6,10},{7,11},{8,12},{9,13},{1... | collective-permute-start | bytes 835592 | tf_op jit(solution)/shard_map/ppermute | solution.py:315
  12.0 3.3 %collective-permute-start.2 = (bf16[256,512]{1,0:T(8,128)(2,1)S(1)}, bf16[256,512]{1,0:T(8,128)(2,1)S(1)}, u32[]{:S(2)}, u32[]{:S(2)}) collective-permute-start(bf16[256,512]{1,0:T(8,128)(2,1)S(1)} %slice_select_fusion.1), channel_id=1, source_target_pairs={{0,1},{1,0},{2,3},{3,2},{4,5},{5,4},{6,7},{7,6},{8,9},{9,8},{10,11... | collective-permute-start | bytes 786440 | tf_op jit(solution)/shard_map/ppermute | solution.py:326
  18.4 2.4 %collective-permute-start.3 = (bf16[256,512]{1,0:T(8,128)(2,1)S(1)}, bf16[256,512]{1,0:T(8,128)(2,1)S(1)}, u32[]{:S(2)}, u32[]{:S(2)}) collective-permute-start(bf16[256,512]{1,0:T(8,128)(2,1)S(1)} %slice_select_fusion), channel_id=1, source_target_pairs={{0,1},{1,0},{2,3},{3,2},{4,5},{5,4},{6,7},{7,6},{8,9},{9,8},{10,11... | collective-permute-start | bytes 786440 | tf_op jit(solution)/shard_map/ppermute | solution.py:326

commit v2 on v1

--- a/solution.py
+++ b/solution.py
@@ -13,6 +13,7 @@
 KEY_VALUE_HEADS = 4
 GROUP = QUERY_HEADS // KEY_VALUE_HEADS
 HEADS_AT_ONCE = 4
+EARLY_CHAINS = 4
 EXCLUDED = -1e30
 PAD = 16
 AXES = ("dp", "ctx")
@@ -60,8 +61,7 @@
     ]
 
 
-def in_turn(*stages):
-    runs = chains()
+def in_turn(runs, *stages):
     results = {}
     for turn in range(len(runs) + len(stages) - 1):
         for n, stage in enumerate(stages):
@@ -70,13 +70,12 @@
                 results[i] = stage(*runs[i], *results.pop(i, ()))
 
 
-def pack_kernel(key_hbm, value_hbm, *refs):
-    *outs, sems = refs
+def pack_kernel(key_hbm, value_hbm, out_ref, sems):
     rows = key_hbm.shape[0]
-    copies = []
-    for n, out in enumerate(outs):
-        copies.append(pltpu.make_async_copy(key_hbm, out.at[:rows], sems.at[n, 0]))
-        copies.append(pltpu.make_async_copy(value_hbm, out.at[rows : 2 * rows], sems.at[n, 1]))
+    copies = [
+        pltpu.make_async_copy(key_hbm, out_ref.at[:rows], sems.at[0]),
+        pltpu.make_async_copy(value_hbm, out_ref.at[rows:], sems.at[1]),
+    ]
     for copy in copies:
         copy.start()
     for copy in copies:
@@ -85,22 +84,40 @@
 
 def pack(keys, values):
     rows, width = keys.shape
-    packed = pltpu.VMEM((2 * rows, width), keys.dtype)
-    longer = pltpu.VMEM((2 * rows + PAD, width), keys.dtype)
     return pl.pallas_call(
         pack_kernel,
-        out_shape=(packed, longer),
+        out_shape=pltpu.VMEM((2 * rows, width), keys.dtype),
         in_specs=[HBM, HBM],
-        out_specs=(VMEM, VMEM),
-        scratch_shapes=[pltpu.SemaphoreType.DMA((2, 2))],
+        out_specs=VMEM,
+        scratch_shapes=[pltpu.SemaphoreType.DMA((2,))],
         compiler_params=pltpu.CompilerParams(vmem_limit_bytes=1024 * 1024),
     )(*in_hbm(keys, values))
 
 
+def attend_own(runs, rows, own_ref, own_bias_ref, q_ref, top_ref, total_ref, sum_ref, ready):
+    def match(heads, g):
+        ready(heads, g)
+        key = own_ref[:rows, head_columns(g)]
+        return (scores_of(stacked(q_ref, heads), key, own_bias_ref[...]),)
+
+    def weigh(heads, g, scores):
+        top = jnp.max(scores, axis=1, keepdims=True)
+        spread(top_ref, heads, rows, jnp.broadcast_to(top, scores.shape))
+        return (weights_of(scores, top),)
+
+    def gather(heads, g, weights):
+        value = with_ones(own_ref[rows:, head_columns(g)])
+        summed = jnp.dot(weights, value, preferred_element_type=jnp.float32)
+        spread(sum_ref, heads, rows, summed[:, :HEAD_SIZE])
+        spread(total_ref, heads, rows, summed[:, HEAD_SIZE:])
+
+    in_turn(runs, match, weigh, gather)
+
+
 def own_kernel(
     rounds, rows, own_ref, lengths_hbm, q_hbm,
-    longer_ref, bias_ref, needed_ref, odd_ref, q_ref, top_ref, total_ref, sum_ref,
-    own_bias_ref, lengths_ref, lengths_sem, q_sems,
+    longer_ref, bias_ref, needed_ref, own_bias_ref, q_ref, odd_ref, top_ref, total_ref, sum_ref,
+    lengths_ref, lengths_sem, q_sems,
 ):
     lengths_copy = pltpu.make_async_copy(lengths_hbm, lengths_ref, lengths_sem)
     lengths_copy.start()
@@ -111,6 +128,7 @@
         q_copies.append(pltpu.make_async_copy(q_hbm.at[:, at], q_ref.at[:, at], q_sems.at[g]))
         q_copies[g].start()
     me = lax.axis_index("dp") * lax.axis_size("ctx") + lax.axis_index("ctx")
+    longer_ref[: 2 * rows, :] = own_ref[...]
     longer_ref[2 * rows :, :] = jnp.zeros((PAD, longer_ref.shape[1]), longer_ref.dtype)
     odd_ref[...] = jnp.full(odd_ref.shape, lax.rem(me, 2), jnp.int32)
     first = me * rows
@@ -144,23 +162,22 @@
         key_pos = first - (b + 1) * rows + lane
         bias_ref[:, b * rows : (b + 1) * rows] = bias_of(key_pos >= start)
 
-    def match(heads, g):
+    def ready(heads, g):
         if heads[0] % GROUP == 0:
             q_copies[g].wait()
-        return (scores_of(stacked(q_ref, heads), own_ref[:rows, head_columns(g)], own_bias_ref[...]),)
-
-    def weigh(heads, g, scores):
-        top = jnp.max(scores, axis=1, keepdims=True)
-        spread(top_ref, heads, rows, jnp.broadcast_to(top, scores.shape))
-        return (weights_of(scores, top),)
-
-    def gather(heads, g, weights):
-        value = with_ones(own_ref[rows : 2 * rows, head_columns(g)])
-        summed = jnp.dot(weights, value, preferred_element_type=jnp.float32)
-        spread(sum_ref, heads, rows, summed[:, :HEAD_SIZE])
-        spread(total_ref, heads, rows, summed[:, HEAD_SIZE:])
-
-    in_turn(match, weigh, gather)
+
+    runs = chains()[:EARLY_CHAINS]
+    attend_own(runs, rows, own_ref, own_bias_ref, q_ref, top_ref, total_ref, sum_ref, ready)
+    for copy in q_copies[runs[-1][1] + 1 :]:
+        copy.wait()
+
+
+def own_rest_kernel(
+    rows, own_ref, own_bias_ref, q_ref, odd_ref, *parts
+):
+    runs = chains()[EARLY_CHAINS:]
+    parts = parts[4:]
+    attend_own(runs, rows, own_ref, own_bias_ref, q_ref, *parts, lambda heads, g: None)
 
 
 def in_vmem(*operands):
@@ -178,24 +195,23 @@
 
 def own_part(lengths, queries, own, rounds):
     rows = queries.shape[0]
-    partial = pltpu.VMEM(queries.shape, jnp.float32)
+    part = pltpu.VMEM(queries.shape, jnp.float32)
     return pl.pallas_call(
         functools.partial(own_kernel, rounds, rows),
         out_shape=(
-            pltpu.VMEM(own.shape, own.dtype),
+            pltpu.VMEM((2 * rows + PAD, own.shape[1]), own.dtype),
             pltpu.VMEM((rows, 2 * rounds * rows), jnp.float32),
             pltpu.VMEM((8, 128), jnp.int32),
+            pltpu.VMEM((rows, rows), jnp.float32),
+            pltpu.VMEM(queries.shape, queries.dtype),
             pltpu.VMEM((1, own.shape[1]), jnp.int32),
-            pltpu.VMEM(queries.shape, queries.dtype),
-            partial,
-            partial,
-            partial,
+            part,
+            part,
+            part,
         ),
         in_specs=[VMEM, HBM, HBM],
-        out_specs=(VMEM,) * 8,
-        input_output_aliases={0: 0},
+        out_specs=(VMEM,) * 9,
         scratch_shapes=[
-            pltpu.VMEM((rows, rows), jnp.float32),
             pltpu.SMEM(lengths.shape, jnp.int32),
             pltpu.SemaphoreType.DMA,
             pltpu.SemaphoreType.DMA((KEY_VALUE_HEADS,)),
@@ -207,18 +223,34 @@
     )(*in_vmem(own), *in_hbm(lengths, queries))
 
 
+def own_rest(own, own_bias, queries, kept):
+    rows = queries.shape[0]
+    operands = in_vmem(own, own_bias, queries, *kept)
+    return pl.pallas_call(
+        functools.partial(own_rest_kernel, rows),
+        out_shape=tuple(pltpu.VMEM(x.shape, x.dtype) for x in kept),
+        in_specs=[VMEM] * len(operands),
+        out_specs=(VMEM,) * len(kept),
+        input_output_aliases={3 + n: n for n in range(len(kept))},
+        compiler_params=pltpu.CompilerParams(vmem_limit_bytes=10 * 1024 * 1024),
+        cost_estimate=pl.CostEstimate(
+            flops=4 * 10**9, bytes_accessed=16 * 10**6, transcendentals=rows * queries.size
+        ),
+    )(*operands)
+
+
 def behind_kernel(
     before, last, rows, needed_ref, bias_ref, q_ref, near_ref, further_ref, top_ref, total_ref, sum_ref, *refs
 ):
-    width = GROUP * HEAD_SIZE
     beyond = needed_ref[0, 0] - before
     pairs = [(ref.at[:rows], ref.at[rows : 2 * rows]) for ref in (near_ref, further_ref)]
     if last:
         out_hbm, out_ref, out_sems = refs
 
-        def out_copy(g):
-            at = slice(g * width, (g + 1) * width)
-            return pltpu.make_async_copy(out_ref.at[:, at], out_hbm.at[:, at], out_sems.at[g])
+        def out_copy(n):
+            width = HEADS_AT_ONCE * HEAD_SIZE
+            at = slice(n * width, (n + 1) * width)
+            return pltpu.make_async_copy(out_ref.at[:, at], out_hbm.at[:, at], out_sems.at[n])
 
     else:
         _, new_top_ref, new_total_ref, new_sum_ref = refs
@@ -226,8 +258,7 @@
     def finish(heads, g, summed, total):
         if last:
             spread(out_ref, heads, rows, normalised(summed, total))
-            if heads[-1] % GROUP == GROUP - 1:
-                out_copy(g).start()
+            out_copy(heads[0] // HEADS_AT_ONCE).start()
         else:
             spread(new_sum_ref, heads, rows, summed)
             spread(new_total_ref, heads, rows, total)
@@ -253,7 +284,7 @@
             total = stacked(total_ref, heads) * fade + more[:, HEAD_SIZE:]
             finish(heads, g, summed, total)
 
-        in_turn(match, weigh, gather)
+        in_turn(chains(), match, weigh, gather)
 
     @pl.when(beyond > 1)
     def _():
@@ -267,11 +298,12 @@
         @pl.when(beyond < 1)
         def _():
             in_turn(
-                lambda heads, g: finish(heads, g, stacked(sum_ref, heads), stacked(total_ref, heads))
+                chains(),
+                lambda heads, g: finish(heads, g, stacked(sum_ref, heads), stacked(total_ref, heads)),
             )
 
-        for g in range(KEY_VALUE_HEADS):
-            out_copy(g).wait()
+        for n in range(len(chains())):
+            out_copy(n).wait()
 
 
 def behind_part(before, last, needed, bias, queries, near, further, parts):
@@ -283,7 +315,7 @@
         out_specs = HBM
         scratch = [
             pltpu.VMEM(queries.shape, queries.dtype),
-            pltpu.SemaphoreType.DMA((KEY_VALUE_HEADS,)),
+            pltpu.SemaphoreType.DMA((len(chains()),)),
         ]
         aliases = {}
     else:
@@ -314,10 +346,11 @@
         by = 2 * (r + 1)
         return lax.ppermute(block, AXES, [(i, i + by) for i in range(count - by)])
 
-    packed, own = pack(keys, values)
-    fetched = [from_behind(packed, 0)]
-    own, bias, needed, odd, queries, *parts = own_part(lengths, queries, own, rounds)
-    fetched += [from_behind(own, r) for r in range(1, rounds)]
+    own = pack(keys, values)
+    fetched = [from_behind(own, 0)]
+    longer, bias, needed, own_bias, queries, *kept = own_part(lengths, queries, own, rounds)
+    fetched += [from_behind(longer, r) for r in range(1, rounds)]
+    odd, *parts = own_rest(own, own_bias, queries, kept)
     swap = [(i, i ^ 1) for i in range(count)]
     nearer = own
     size = 2 * keys.shape[0]

time: 24 us -> 24.2 us (level)
  the two profiles are of different devices: /device:TPU:25 before, /device:TPU:9 now
where the time goes in v2:
time: 24.2 us; the launch traced here: 24.1 us
  Pallas kernels  10 us (41%)
  starting transfers between devices  9.76 us (40%)
  waiting for transfers between devices  4.19 us (17%)
    pallas_call x2, Pallas kernels, behind_part(): pl.pallas_call(functools.partial(behind_kernel, before, last, rows), out_...  6.36 us
    ppermute x2, starting transfers between devices, from_behind(): return lax.ppermute(block, AXES, [(i, i + by) for i in range(count - by)])  6.27 us
    ppermute x2, starting transfers between devices, per_device(): lax.ppermute(jnp.where(odd == 1, further[:size], nearer[:size]), AXES, swap)  3.49 us
    ppermute x2, waiting for transfers between devices, per_device(): lax.ppermute(jnp.where(odd == 1, further[:size], nearer[:size]), AXES, swap)  2.32 us
    pallas_call x1, Pallas kernels, own_part(): pl.pallas_call(functools.partial(own_kernel, rounds, rows), out_shape=(pl...  1.95 us
    ppermute x2, waiting for transfers between devices, from_behind(): return lax.ppermute(block, AXES, [(i, i + by) for i in range(count - by)])  1.86 us
    pallas_call x1, Pallas kernels, pack(): pl.pallas_call(pack_kernel, out_shape=pltpu.VMEM((2 * rows, width), keys....  0.98 us
    pallas_call x1, Pallas kernels, own_rest(): pl.pallas_call(functools.partial(own_rest_kernel, rows), out_shape=tuple(...  0.73 us
  transfers between devices with their start and end apart: 4, of which 3 were waited for; matrix products, arithmetic and copies ran while one was open for 0% of the time, Pallas kernels for 24%

profile of v2, /device:TPU:9, one launch (start us, length us, event | category | flops | bytes accessed | tf_op | source)
XLA Modules:
  0.0 24.1 jit_solution(3347848107042744261)
XLA Ops:
  0.0 1.0 %shard_map.46.own_ref = bf16[256,512]{1,0:T(8,128)(2,1)S(1)} custom-call(bf16[128,512]{1,0:T(8,128)(2,1)} %key_hbm.1, bf16[128,512]{1,0:T(8,128)(2,1)} %value_hbm.1), custom_call_target="tpu_custom_call" | custom-call | tf_op jit(solution)/shard_map/pallas_call | solution.py:87
  1.0 3.1 %collective-permute-start.1 = (bf16[256,512]{1,0:T(8,128)(2,1)S(1)}, bf16[256,512]{1,0:T(8,128)(2,1)S(1)}, u32[]{:S(2)}, u32[]{:S(2)}) collective-permute-start(bf16[256,512]{1,0:T(8,128)(2,1)S(1)} %shard_map.46.own_ref), channel_id=1, source_target_pairs={{0,2},{1,3},{2,4},{3,5},{4,6},{5,7},{6,8},{7,9},{8,10},{9,11},{10,... | collective-permute-start | bytes 786440 | tf_op jit(solution)/shard_map/ppermute | solution.py:347
  4.1 2.0 %shard_map.47 = (bf16[272,512]{1,0:T(8,128)(2,1)S(1)}, f32[128,512]{1,0:T(8,128)S(1)}, s32[8,128]{1,0:T(8,128)S(1)}, f32[128,128]{1,0:T(8,128)S(1)}, bf16[128,40...) custom-call(bf16[256,512]{1,0:T(8,128)(2,1)S(1)} %shard_map.46.own_r, ...), custom_call_target="tpu_custom_call" | custom-call | flops 4000000000 | bytes 16000000 | tf_op jit(solution)/shard_map/pallas_call | solution.py:199
  6.1 3.1 %collective-permute-start = (bf16[272,512]{1,0:T(8,128)(2,1)S(1)}, bf16[272,512]{1,0:T(8,128)(2,1)S(1)}, u32[]{:S(2)}, u32[]{:S(2)}) collective-permute-start(bf16[272,512]{1,0:T(8,128)(2,1)S(1)} %get-tuple-element.31), channel_id=1, source_target_pairs={{0,4},{1,5},{2,6},{3,7},{4,8},{5,9},{6,10},{7,11},{8,12},{9,13},{1... | collective-permute-start | bytes 835592 | tf_op jit(solution)/shard_map/ppermute | solution.py:347
  9.2 0.7 %shard_map.48 = (s32[1,512]{1,0:T(1,128)S(1)}, f32[128,4096]{1,0:T(8,128)S(1)}, f32[128,4096]{1,0:T(8,128)S(1)}, f32[128,4096]{1,0:T(8,128)S(1)}) custom-call(bf16[256,512]{1,0:T(8,128)(2,1)S(1)} %shard_map.46.own_ref, f32[128,128]{1,0:T(8,128)S(1)} %get-tuple-element.25.own_bias_ref, ...), custom_call_target="tpu_custom_call", output_to_operand_aliasing={{0}: (3, {}), {1}: (4, {}), {2}: (5, {}), {3}: (6, {})} | custom-call | flops 4000000000 | bytes 16000000 | tf_op jit(solution)/shard_map/pallas_call | solution.py:229
  10.0 1.9 %collective-permute-done.1.further_ref = bf16[256,512]{1,0:T(8,128)(2,1)S(1)} collective-permute-done((bf16[256,512]{1,0:T(8,128)(2,1)S(1)}, bf16[256,512]{1,0:T(8,128)(2,1)S(1)}, u32[]{:S(2)}, u32[]{:S(2)}) %collective-permute-start.1) | collective-permute-done | bytes 262176 | tf_op jit(solution)/shard_map/ppermute | solution.py:347
  11.9 3.0 %collective-permute-start.2 = (bf16[256,512]{1,0:T(8,128)(2,1)S(1)}, bf16[256,512]{1,0:T(8,128)(2,1)S(1)}, u32[]{:S(2)}, u32[]{:S(2)}) collective-permute-start(bf16[256,512]{1,0:T(8,128)(2,1)S(1)} %broadcast_select_fusion), channel_id=1, source_target_pairs={{0,1},{1,0},{2,3},{3,2},{4,5},{5,4},{6,7},{7,6},{8,9},{9,8},{10,11... | collective-permute-start | bytes 786440 | tf_op jit(solution)/shard_map/ppermute | solution.py:359
  14.9 1.2 %collective-permute-done.2.near_ref = bf16[256,512]{1,0:T(8,128)(2,1)S(1)} collective-permute-done((bf16[256,512]{1,0:T(8,128)(2,1)S(1)}, bf16[256,512]{1,0:T(8,128)(2,1)S(1)}, u32[]{:S(2)}, u32[]{:S(2)}) %collective-permute-start.2) | collective-permute-done | bytes 262176 | tf_op jit(solution)/shard_map/ppermute | solution.py:359
  16.1 3.0 %shard_map.49 = (bf16[256,512]{1,0:T(8,128)(2,1)S(1)}, f32[128,4096]{1,0:T(8,128)S(1)}, f32[128,4096]{1,0:T(8,128)S(1)}, f32[128,4096]{1,0:T(8,128)S(1)}) custom-call(s32[8,128]{1,0:T(8,128)S(1)} %get-tuple-element.22.needed_ref, f32[128,512]{1,0:T(8,128)S(1)} %get-tuple-element.23.bias_ref, ...), custom_call_target="tpu_custom_call", output_to_operand_aliasing={{0}: (4, {}), {1}: (5, {}), {2}: (6, {}), {3}: (7, {})} | custom-call | flops 4194304 | bytes 524288 | tf_op jit(solution)/shard_map/pallas_call | solution.py:327
  19.1 0.0 collective-permute-done.further_ref
  19.2 0.4 %collective-permute-start.3 = (bf16[256,512]{1,0:T(8,128)(2,1)S(1)}, bf16[256,512]{1,0:T(8,128)(2,1)S(1)}, u32[]{:S(2)}, u32[]{:S(2)}) collective-permute-start(bf16[256,512]{1,0:T(8,128)(2,1)S(1)} %slice_select_fusion), channel_id=1, source_target_pairs={{0,1},{1,0},{2,3},{3,2},{4,5},{5,4},{6,7},{7,6},{8,9},{9,8},{10,11... | collective-permute-start | bytes 786440 | tf_op jit(solution)/shard_map/ppermute | solution.py:359
  19.6 1.2 %collective-permute-done.3.near_ref = bf16[256,512]{1,0:T(8,128)(2,1)S(1)} collective-permute-done((bf16[256,512]{1,0:T(8,128)(2,1)S(1)}, bf16[256,512]{1,0:T(8,128)(2,1)S(1)}, u32[]{:S(2)}, u32[]{:S(2)}) %collective-permute-start.3) | collective-permute-done | bytes 262176 | tf_op jit(solution)/shard_map/ppermute | solution.py:359
  20.8 3.3 %shard_map.50 = bf16[128,4096]{1,0:T(8,128)(2,1)} custom-call(s32[8,128]{1,0:T(8,128)S(1)} %get-tuple-element.22.needed_ref, f32[128,512]{1,0:T(8,128)S(1)} %get-tuple-element.23.bias_ref, bf16[128,4096]{1,0:T(8,128)(2,1)S(1)} %get-tuple-element.24.q_ref, bf16[256,512]{1,0:T(8,128)(2,1)S(1)} %collective-permute-done.3.near_ref, ...), custom_call_target="tpu_custom_call" | custom-call | flops 4194304 | bytes 524288 | tf_op jit(solution)/shard_map/pallas_call | solution.py:327
  (3 shorter events, 0.1 us)
Async XLA Ops:
  1.0 10.9 %collective-permute-start.1 = (bf16[256,512]{1,0:T(8,128)(2,1)S(1)}, bf16[256,512]{1,0:T(8,128)(2,1)S(1)}, u32[]{:S(2)}, u32[]{:S(2)}) collective-permute-start(bf16[256,512]{1,0:T(8,128)(2,1)S(1)} %shard_map.46.own_ref), channel_id=1, source_target_pairs={{0,2},{1,3},{2,4},{3,5},{4,6},{5,7},{6,8},{7,9},{8,10},{9,11},{10,... | collective-permute-start | bytes 786440 | tf_op jit(solution)/shard_map/ppermute | solution.py:347
  6.1 13.1 %collective-permute-start = (bf16[272,512]{1,0:T(8,128)(2,1)S(1)}, bf16[272,512]{1,0:T(8,128)(2,1)S(1)}, u32[]{:S(2)}, u32[]{:S(2)}) collective-permute-start(bf16[272,512]{1,0:T(8,128)(2,1)S(1)} %get-tuple-element.31), channel_id=1, source_target_pairs={{0,4},{1,5},{2,6},{3,7},{4,8},{5,9},{6,10},{7,11},{8,12},{9,13},{1... | collective-permute-start | bytes 835592 | tf_op jit(solution)/shard_map/ppermute | solution.py:347
  11.9 4.2 %collective-permute-start.2 = (bf16[256,512]{1,0:T(8,128)(2,1)S(1)}, bf16[256,512]{1,0:T(8,128)(2,1)S(1)}, u32[]{:S(2)}, u32[]{:S(2)}) collective-permute-start(bf16[256,512]{1,0:T(8,128)(2,1)S(1)} %broadcast_select_fusion), channel_id=1, source_target_pairs={{0,1},{1,0},{2,3},{3,2},{4,5},{5,4},{6,7},{7,6},{8,9},{9,8},{10,11... | collective-permute-start | bytes 786440 | tf_op jit(solution)/shard_map/ppermute | solution.py:359
  19.2 1.6 %collective-permute-start.3 = (bf16[256,512]{1,0:T(8,128)(2,1)S(1)}, bf16[256,512]{1,0:T(8,128)(2,1)S(1)}, u32[]{:S(2)}, u32[]{:S(2)}) collective-permute-start(bf16[256,512]{1,0:T(8,128)(2,1)S(1)} %slice_select_fusion), channel_id=1, source_target_pairs={{0,1},{1,0},{2,3},{3,2},{4,5},{5,4},{6,7},{7,6},{8,9},{9,8},{10,11... | collective-permute-start | bytes 786440 | tf_op jit(solution)/shard_map/ppermute | solution.py:359

commit v3 on v2

--- a/solution.py
+++ b/solution.py
@@ -12,8 +12,8 @@
 QUERY_HEADS = 32
 KEY_VALUE_HEADS = 4
 GROUP = QUERY_HEADS // KEY_VALUE_HEADS
-HEADS_AT_ONCE = 4
-EARLY_CHAINS = 4
+HEADS_AT_ONCE = 8
+EARLY_CHAINS = 2
 EXCLUDED = -1e30
 PAD = 16
 AXES = ("dp", "ctx")

time: 24.2 us -> 23.7 us (0.979)
  the two profiles are of different devices: /device:TPU:9 before, /device:TPU:16 now
where the time goes in v3:
time: 23.7 us; the launch traced here: 23.9 us
  Pallas kernels  10.2 us (43%)
  starting transfers between devices  6.97 us (29%)
  waiting for transfers between devices  6.59 us (28%)
    ppermute x2, starting transfers between devices, from_behind(): return lax.ppermute(block, AXES, [(i, i + by) for i in range(count - by)])  6.83 us
    pallas_call x2, Pallas kernels, behind_part(): pl.pallas_call(functools.partial(behind_kernel, before, last, rows), out_...  6.52 us
    ppermute x2, waiting for transfers between devices, from_behind(): return lax.ppermute(block, AXES, [(i, i + by) for i in range(count - by)])  3.54 us
    ppermute x2, waiting for transfers between devices, per_device(): lax.ppermute(jnp.where(odd == 1, further[:size], nearer[:size]), AXES, swap)  3.04 us
    pallas_call x1, Pallas kernels, own_part(): pl.pallas_call(functools.partial(own_kernel, rounds, rows), out_shape=(pl...  2.01 us
    pallas_call x1, Pallas kernels, pack(): pl.pallas_call(pack_kernel, out_shape=pltpu.VMEM((2 * rows, width), keys....  0.98 us
    pallas_call x1, Pallas kernels, own_rest(): pl.pallas_call(functools.partial(own_rest_kernel, rows), out_shape=tuple(...  0.69 us
  transfers between devices with their start and end apart: 4, of which 3 were waited for; matrix products, arithmetic and copies ran while one was open for 0% of the time, Pallas kernels for 24%

profile of v3, /device:TPU:16, one launch (start us, length us, event | category | flops | bytes accessed | tf_op | source)
XLA Modules:
  0.0 23.9 jit_solution(12816090314523396873)
XLA Ops:
  0.0 1.0 %shard_map.46.own_ref = bf16[256,512]{1,0:T(8,128)(2,1)S(1)} custom-call(bf16[128,512]{1,0:T(8,128)(2,1)} %key_hbm.1, bf16[128,512]{1,0:T(8,128)(2,1)} %value_hbm.1), custom_call_target="tpu_custom_call" | custom-call | tf_op jit(solution)/shard_map/pallas_call | solution.py:87
  1.0 3.4 %collective-permute-start.1 = (bf16[256,512]{1,0:T(8,128)(2,1)S(1)}, bf16[256,512]{1,0:T(8,128)(2,1)S(1)}, u32[]{:S(2)}, u32[]{:S(2)}) collective-permute-start(bf16[256,512]{1,0:T(8,128)(2,1)S(1)} %shard_map.46.own_ref), channel_id=1, source_target_pairs={{0,2},{1,3},{2,4},{3,5},{4,6},{5,7},{6,8},{7,9},{8,10},{9,11},{10,... | collective-permute-start | bytes 786440 | tf_op jit(solution)/shard_map/ppermute | solution.py:347
  4.4 2.0 %shard_map.47 = (bf16[272,512]{1,0:T(8,128)(2,1)S(1)}, f32[128,512]{1,0:T(8,128)S(1)}, s32[8,128]{1,0:T(8,128)S(1)}, f32[128,128]{1,0:T(8,128)S(1)}, bf16[128,40...) custom-call(bf16[256,512]{1,0:T(8,128)(2,1)S(1)} %shard_map.46.own_r, ...), custom_call_target="tpu_custom_call" | custom-call | flops 4000000000 | bytes 16000000 | tf_op jit(solution)/shard_map/pallas_call | solution.py:199
  6.4 3.4 %collective-permute-start = (bf16[272,512]{1,0:T(8,128)(2,1)S(1)}, bf16[272,512]{1,0:T(8,128)(2,1)S(1)}, u32[]{:S(2)}, u32[]{:S(2)}) collective-permute-start(bf16[272,512]{1,0:T(8,128)(2,1)S(1)} %get-tuple-element.31), channel_id=1, source_target_pairs={{0,4},{1,5},{2,6},{3,7},{4,8},{5,9},{6,10},{7,11},{8,12},{9,13},{1... | collective-permute-start | bytes 835592 | tf_op jit(solution)/shard_map/ppermute | solution.py:347
  9.8 0.7 %shard_map.48 = (s32[1,512]{1,0:T(1,128)S(1)}, f32[128,4096]{1,0:T(8,128)S(1)}, f32[128,4096]{1,0:T(8,128)S(1)}, f32[128,4096]{1,0:T(8,128)S(1)}) custom-call(bf16[256,512]{1,0:T(8,128)(2,1)S(1)} %shard_map.46.own_ref, f32[128,128]{1,0:T(8,128)S(1)} %get-tuple-element.25.own_bias_ref, ...), custom_call_target="tpu_custom_call", output_to_operand_aliasing={{0}: (3, {}), {1}: (4, {}), {2}: (5, {}), {3}: (6, {})} | custom-call | flops 4000000000 | bytes 16000000 | tf_op jit(solution)/shard_map/pallas_call | solution.py:229
  10.6 3.5 %collective-permute-done.1.further_ref = bf16[256,512]{1,0:T(8,128)(2,1)S(1)} collective-permute-done((bf16[256,512]{1,0:T(8,128)(2,1)S(1)}, bf16[256,512]{1,0:T(8,128)(2,1)S(1)}, u32[]{:S(2)}, u32[]{:S(2)}) %collective-permute-start.1) | collective-permute-done | bytes 262176 | tf_op jit(solution)/shard_map/ppermute | solution.py:347
  14.1 0.1 collective-permute-start.2
  14.2 1.5 %collective-permute-done.2.near_ref = bf16[256,512]{1,0:T(8,128)(2,1)S(1)} collective-permute-done((bf16[256,512]{1,0:T(8,128)(2,1)S(1)}, bf16[256,512]{1,0:T(8,128)(2,1)S(1)}, u32[]{:S(2)}, u32[]{:S(2)}) %collective-permute-start.2) | collective-permute-done | bytes 262176 | tf_op jit(solution)/shard_map/ppermute | solution.py:359
  15.7 3.1 %shard_map.49 = (bf16[256,512]{1,0:T(8,128)(2,1)S(1)}, f32[128,4096]{1,0:T(8,128)S(1)}, f32[128,4096]{1,0:T(8,128)S(1)}, f32[128,4096]{1,0:T(8,128)S(1)}) custom-call(s32[8,128]{1,0:T(8,128)S(1)} %get-tuple-element.22.needed_ref, f32[128,512]{1,0:T(8,128)S(1)} %get-tuple-element.23.bias_ref, ...), custom_call_target="tpu_custom_call", output_to_operand_aliasing={{0}: (4, {}), {1}: (5, {}), {2}: (6, {}), {3}: (7, {})} | custom-call | flops 4194304 | bytes 524288 | tf_op jit(solution)/shard_map/pallas_call | solution.py:327
  18.8 0.0 collective-permute-done.further_ref
  18.9 0.1 collective-permute-start.3
  19.0 1.5 %collective-permute-done.3.near_ref = bf16[256,512]{1,0:T(8,128)(2,1)S(1)} collective-permute-done((bf16[256,512]{1,0:T(8,128)(2,1)S(1)}, bf16[256,512]{1,0:T(8,128)(2,1)S(1)}, u32[]{:S(2)}, u32[]{:S(2)}) %collective-permute-start.3) | collective-permute-done | bytes 262176 | tf_op jit(solution)/shard_map/ppermute | solution.py:359
  20.5 3.4 %shard_map.50 = bf16[128,4096]{1,0:T(8,128)(2,1)} custom-call(s32[8,128]{1,0:T(8,128)S(1)} %get-tuple-element.22.needed_ref, f32[128,512]{1,0:T(8,128)S(1)} %get-tuple-element.23.bias_ref, bf16[128,4096]{1,0:T(8,128)(2,1)S(1)} %get-tuple-element.24.q_ref, bf16[256,512]{1,0:T(8,128)(2,1)S(1)} %collective-permute-done.3.near_ref, ...), custom_call_target="tpu_custom_call" | custom-call | flops 4194304 | bytes 524288 | tf_op jit(solution)/shard_map/pallas_call | solution.py:327
  (3 shorter events, 0.1 us)
Async XLA Ops:
  1.0 13.1 %collective-permute-start.1 = (bf16[256,512]{1,0:T(8,128)(2,1)S(1)}, bf16[256,512]{1,0:T(8,128)(2,1)S(1)}, u32[]{:S(2)}, u32[]{:S(2)}) collective-permute-start(bf16[256,512]{1,0:T(8,128)(2,1)S(1)} %shard_map.46.own_ref), channel_id=1, source_target_pairs={{0,2},{1,3},{2,4},{3,5},{4,6},{5,7},{6,8},{7,9},{8,10},{9,11},{10,... | collective-permute-start | bytes 786440 | tf_op jit(solution)/shard_map/ppermute | solution.py:347
  6.4 12.4 %collective-permute-start = (bf16[272,512]{1,0:T(8,128)(2,1)S(1)}, bf16[272,512]{1,0:T(8,128)(2,1)S(1)}, u32[]{:S(2)}, u32[]{:S(2)}) collective-permute-start(bf16[272,512]{1,0:T(8,128)(2,1)S(1)} %get-tuple-element.31), channel_id=1, source_target_pairs={{0,4},{1,5},{2,6},{3,7},{4,8},{5,9},{6,10},{7,11},{8,12},{9,13},{1... | collective-permute-start | bytes 835592 | tf_op jit(solution)/shard_map/ppermute | solution.py:347
  14.1 1.6 %collective-permute-start.2 = (bf16[256,512]{1,0:T(8,128)(2,1)S(1)}, bf16[256,512]{1,0:T(8,128)(2,1)S(1)}, u32[]{:S(2)}, u32[]{:S(2)}) collective-permute-start(bf16[256,512]{1,0:T(8,128)(2,1)S(1)} %broadcast_select_fusion), channel_id=1, source_target_pairs={{0,1},{1,0},{2,3},{3,2},{4,5},{5,4},{6,7},{7,6},{8,9},{9,8},{10,11... | collective-permute-start | bytes 786440 | tf_op jit(solution)/shard_map/ppermute | solution.py:359
  18.9 1.6 %collective-permute-start.3 = (bf16[256,512]{1,0:T(8,128)(2,1)S(1)}, bf16[256,512]{1,0:T(8,128)(2,1)S(1)}, u32[]{:S(2)}, u32[]{:S(2)}) collective-permute-start(bf16[256,512]{1,0:T(8,128)(2,1)S(1)} %slice_select_fusion), channel_id=1, source_target_pairs={{0,1},{1,0},{2,3},{3,2},{4,5},{5,4},{6,7},{7,6},{8,9},{9,8},{10,11... | collective-permute-start | bytes 786440 | tf_op jit(solution)/shard_map/ppermute | solution.py:359
